TPU v7x, 128 devices: a whole 4x4x4 slice. The times are simulated.
128 devices in a mesh: cp: 64 (over y, x, z), grp: 2 (over core).
Axes of the slice: x: 4, y: 4, z: 4, core: 2. Of those that a mesh axis runs over, the one named last changes fastest.
Arguments:
- queries: bfloat16 [16384, 640], P(('cp', 'grp')), may hold values from -24 to 24
- attn_keys: bfloat16 [16384, 128], P(('cp', 'grp')), may hold values from -24 to 24
- attn_values: bfloat16 [16384, 128], P(('cp', 'grp')), may hold values from -6 to 6
- out_grad: bfloat16 [16384, 640], P(('cp', 'grp')), may hold values from -6 to 6
- mask_ranges: int32 [13, 5], replicated, may hold values from 0 to 16384, as said below
- span_ids: int32 [256], replicated, may hold values from 0 to 255, as said below
Outputs:
- attn_out: bfloat16 [16384, 640], P(('cp', 'grp'))
- query_grad: bfloat16 [16384, 640], P(('cp', 'grp'))
- key_grad: bfloat16 [16384, 128], P(('cp', 'grp'))
- value_grad: bfloat16 [16384, 128], P(('cp', 'grp'))
Inputs may be any that keep to these rules, and one draw needn't show every extreme that they name: `mask_ranges`: rows 0 to 3 are documents (b, e, b, e, 0) that tile the sequence in order, the first one the shared prefix; row 4 is (p, 16384, 0, p, 1) with p the prefix's end; the last 8 rows are images (s, s + 256, s, s + 256, 1). `span_ids`: each span appears once; the two span slots of one device hold spans c and 255 - c, in either order.
All inputs are finite; a program needn't handle non-finite values.
Results may differ from a plain program's by a relative error of at most 0.014.
Values may be sent and summed in bfloat16 or wider, within the bound.
No kernel may reach another device: no remote copies, remote signals or barrier semaphores. Data moves between devices by JAX's collectives and lax.ppermute only.
A program may use at most 128 MiB of HBM per device.

v0:
```python
import functools
import math

import jax
import jax.numpy as jnp
from jax import lax
from jax.experimental import pallas as pl
from jax.experimental.pallas import tpu as pltpu
from jax.sharding import PartitionSpec as P

SIDE = 4
SPAN = 64
HEADS = 5
DIM = 128
PAIR = 2 * SPAN
LANES = HEADS * PAIR
PAIRS = 2 * SIDE
TILE = 128
TILE_SPANS = TILE // SPAN
PLANE = SIDE * SIDE
KEYS = PLANE * PAIR
KEY_SPANS = KEYS // SPAN
TILES = KEYS // TILE
STAT_ROWS = 2 * PAIRS
WIDTH = HEADS * DIM
GROUPS = (slice(0, 256), slice(256, 512), slice(512, 640))
FAR = -1e30
SCALE = 1.0 / math.sqrt(DIM)
LOG2_SCALE = SCALE * math.log2(math.e)
SHIFTS = (0, 1, -1, 2)
NN = (((1,), (0,)), ((), ()))
NT = (((1,), (1,)), ((), ()))


def dot(a, b, dims=NN):
    return lax.dot_general(a, b, dims, preferred_element_type=jnp.float32)


def flip(a):
    return jnp.transpose(a.astype(jnp.float32))


def rows_of(tile):
    return pl.ds(pl.multiple_of(tile * TILE, TILE), TILE)


def span_rows(ids, first, count, width):
    within = lax.broadcasted_iota(jnp.int32, (SPAN, width), 0)
    return jnp.concatenate([within + ids[first + s] * SPAN for s in range(count)], axis=0)


def seen(tile, key_ids, pair, ranges, query_feature, query_at):
    key_at = span_rows(key_ids, tile * TILE_SPANS, TILE_SPANS, PAIR)
    holds = (key_at >= ranges[0:1, :]) & (key_at < ranges[1:2, :])
    cover = dot(jnp.where(holds, 1.0, 0.0).astype(jnp.bfloat16), query_feature[pair])
    seen = cover > jnp.where(key_at <= query_at[pair, 0:1, :], 0.5, 63.5)
    return jnp.where(seen, 0.0, FAR)


def set_features(query_ids, ranges, query_feature, query_at):
    for pair in range(PAIRS):
        at = span_rows(query_ids, 2 * pair, 2, PAIR)
        holds = (at >= ranges[2:3, :]) & (at < ranges[3:4, :])
        weight = jnp.where(ranges[4:5, :] == 1, 64.0, 1.0)
        query_feature[pair] = flip(jnp.where(holds, weight, 0.0)).astype(jnp.bfloat16)
        query_at[pair] = jnp.transpose(at)[0:8, :]


def walk(order, counts, pair, step):
    whole, some = counts[2 * pair], counts[2 * pair + 1]

    def run(masked, size, first, steps):
        def body(i, _):
            at = pair * TILES + first + i * size
            step(masked, [order[at + t] for t in range(size)])
            return 0

        lax.fori_loop(0, steps, body, 0)
        return first + steps * size

    done = run(False, 4, 0, whole // 4)
    done = run(True, 4, done, (some - done) // 4)
    for size in (3, 2, 1):
        run(True, size, done, jnp.where(some - done == size, 1, 0))


def stack(ref, tiles):
    return jnp.concatenate([ref[rows_of(tile), :] for tile in tiles], axis=0)


def mask_of(tiles, *where):
    return jnp.concatenate([seen(tile, *where) for tile in tiles], axis=0)


def hide(mask, scores, heads):
    return scores + jnp.concatenate([mask] * heads, axis=1)


def pack_kernel(queries, out_grad, keys, values, qg, kv, row, sems):
    copies = [
        pltpu.make_async_copy(keys, row.at[:, :DIM], sems.at[0]),
        pltpu.make_async_copy(values, row.at[:, DIM:], sems.at[1]),
        pltpu.make_async_copy(queries, qg.at[:, :WIDTH], sems.at[2]),
        pltpu.make_async_copy(out_grad, qg.at[:, WIDTH:], sems.at[3]),
    ]
    for copy in copies:
        copy.start()
    for copy in copies[:2]:
        copy.wait()
    for i in range(PLANE):
        kv[i] = row[...]
    for copy in copies[2:]:
        copy.wait()


def join_kernel(a, b, c0, c1, c2, c3):
    for i, c in enumerate((c0, c1, c2, c3)):
        c[...] = (a[i].astype(jnp.float32) + b[i].astype(jnp.float32)).astype(jnp.bfloat16)


def finish_kernel(a0, a1, a2, a3, terms, out, query_grad, key_grad, value_grad):
    for at, to in ((0, out), (WIDTH, query_grad)):
        parts = [a[:, at:at + WIDTH].astype(jnp.float32) for a in (a0, a1, a2, a3)]
        to[...] = sum(parts).astype(jnp.bfloat16)
    for at, to in ((0, key_grad), (DIM, value_grad)):
        parts = [terms[i, :, at:at + DIM].astype(jnp.float32) for i in range(PLANE)]
        to[...] = sum(parts).astype(jnp.bfloat16)


def forward_kernel(
    order, counts, key_ids, key_rank, query_ids, query_rank,
    qg0, qg1, qg2, qg3, qg4, qg5, qg6, qg7, kv, ranges,
    total_out, top_out, stat_out, q_sorted, g_sorted, k_sorted, v_sorted,
    v_turned, stat, query_feature, query_at,
):
    set_features(query_ids, ranges, query_feature, query_at)
    for r, qg in enumerate((qg0, qg1, qg2, qg3, qg4, qg5, qg6, qg7)):
        for s in range(2):
            rank = query_rank[2 * r + s]
            pair, half = rank // 2, lax.rem(rank, 2)
            for h in range(HEADS):
                to = pl.ds(pl.multiple_of(h * PAIR + half * SPAN, SPAN), SPAN)
                q_at, g_at = h * DIM, (HEADS + h) * DIM
                q_sorted[pair, to, :] = qg[s * SPAN:(s + 1) * SPAN, q_at:q_at + DIM]
                g_sorted[pair, to, :] = qg[s * SPAN:(s + 1) * SPAN, g_at:g_at + DIM]

    def sort_keys(i, _):
        for s in range(2):
            rank = key_rank[2 * i + s]
            to = pl.ds(pl.multiple_of(rank * SPAN, SPAN), SPAN)
            rows = kv[i, s * SPAN:(s + 1) * SPAN, :]
            k_sorted[to, :] = rows[:, :DIM]
            v_sorted[to, :] = rows[:, DIM:]
        return 0

    lax.fori_loop(0, PLANE, sort_keys, 0)
    for t in range(TILES):
        v_turned[t] = jnp.transpose(v_sorted[t * TILE:(t + 1) * TILE, :])

    def one_pair(pair, _):
        total_out[pair] = jnp.zeros((DIM, LANES), jnp.float32)
        stat[0:1, :] = jnp.full((1, LANES), FAR, jnp.float32)
        stat[1:2, :] = jnp.zeros((1, LANES), jnp.float32)

        def step(masked, tiles):
            keys = stack(k_sorted, tiles)
            values = jnp.concatenate([v_turned[tile] for tile in tiles], axis=1)
            if masked:
                mask = mask_of(tiles, key_ids, pair, ranges, query_feature, query_at)
            raw = dot(keys, q_sorted[pair, GROUPS[0], :], NT)
            for i, group in enumerate(GROUPS):
                scores = raw * LOG2_SCALE
                if i + 1 < len(GROUPS):
                    raw = dot(keys, q_sorted[pair, GROUPS[i + 1], :], NT)
                if masked:
                    scores = hide(mask, scores, (group.stop - group.start) // PAIR)
                old = stat[0:1, group]
                new = jnp.maximum(old, jnp.max(scores, axis=0, keepdims=True))
                terms = jnp.exp2(scores - new)
                fade = jnp.exp2(old - new)
                stat[0:1, group] = new
                stat[1:2, group] = stat[1:2, group] * fade + jnp.sum(terms, axis=0, keepdims=True)
                total_out[pair, :, group] = total_out[pair, :, group] * fade + dot(
                    values, terms.astype(jnp.bfloat16)
                )

        walk(order, counts, pair, step)
        for h in range(HEADS):
            at = slice(h * PAIR, (h + 1) * PAIR)
            grad = jnp.transpose(g_sorted[pair, at, :]).astype(jnp.float32)
            stat[2:3, at] = jnp.sum(grad * total_out[pair, :, at], axis=0, keepdims=True)
        top, mass = stat[0:1, :], jnp.maximum(stat[1:2, :], 1e-30)
        top_out[pl.ds(pair, 1), :] = top
        stat_out[pl.ds(pair, 1), :] = top + jnp.log2(mass)
        stat_out[pl.ds(PAIRS + pair, 1), :] = stat[2:3, :] / mass
        return 0

    lax.fori_loop(0, PAIRS, one_pair, 0)


def merge(parts):
    logs, leans = [[part[k * PAIRS:(k + 1) * PAIRS, :] for part in parts] for k in range(2)]
    top = functools.reduce(jnp.maximum, logs)
    masses = [jnp.exp2(one - top) for one in logs]
    mass = sum(masses)
    lean = sum(one * part for one, part in zip(leans, masses))
    return top + jnp.log2(mass), lean / mass


def merge_kernel(s0, s1, s2, s3, out):
    for kind, rows in enumerate(merge([s0, s1, s2, s3])):
        out[kind * PAIRS:(kind + 1) * PAIRS, :] = rows


def turn_kernel(k_sorted, k_turned):
    for t in range(TILES):
        k_turned[t] = jnp.transpose(k_sorted[t * TILE:(t + 1) * TILE, :])


def give_back(query_rank, rows, outs, column):
    for r, out in enumerate(outs):
        for s in range(2):
            rank = query_rank[2 * r + s]
            at = pl.ds(pl.multiple_of(lax.rem(rank, 2) * SPAN, SPAN), SPAN)
            out[s * SPAN:(s + 1) * SPAN, column:column + WIDTH] = rows[rank // 2, at, :]


def backward_kernel(
    order, counts, key_ids, key_rank, query_ids, query_rank,
    q_sorted, g_sorted, k_sorted, v_sorted, k_turned, ranges, top_own, stat_mine, stat_other, total,
    od_mine, od_other, kv,
    key_total, value_total, query_total, rows, stat, query_feature, query_at,
):
    set_features(query_ids, ranges, query_feature, query_at)
    outs = [od.at[i] for od in (od_mine, od_other) for i in range(SIDE)]
    log_total, lean = merge([stat_mine, stat_other])
    share = jnp.exp2(top_own[...] - log_total)
    for pair in range(PAIRS):
        stat[pair, 0:1, :] = log_total[pair:pair + 1, :]
        stat[pair, 1:2, :] = lean[pair:pair + 1, :]
        for h in range(HEADS):
            at = slice(h * PAIR, (h + 1) * PAIR)
            scaled = total[pair, :, at] * share[pair:pair + 1, at]
            rows[pair, :, h * DIM:(h + 1) * DIM] = jnp.transpose(scaled.astype(jnp.bfloat16))
    give_back(query_rank, rows, outs, 0)

    query_total[...] = jnp.zeros_like(query_total)
    key_total[...] = jnp.zeros_like(key_total)
    value_total[...] = jnp.zeros_like(value_total)

    def one_pair(pair, _):
        def step(masked, tiles):
            keys, values = stack(k_sorted, tiles), stack(v_sorted, tiles)
            keys_turned = jnp.concatenate([k_turned[tile] for tile in tiles], axis=1)
            if masked:
                mask = mask_of(tiles, key_ids, pair, ranges, query_feature, query_at)

            def products(group):
                return (
                    dot(keys, q_sorted[pair, group, :], NT),
                    dot(values, g_sorted[pair, group, :], NT),
                )

            key_terms, value_terms = 0.0, 0.0
            raw, prob_grad = products(GROUPS[0])
            for i, group in enumerate(GROUPS):
                scores = raw * LOG2_SCALE - stat[pair, 0:1, group]
                lean = prob_grad - stat[pair, 1:2, group]
                if i + 1 < len(GROUPS):
                    raw, prob_grad = products(GROUPS[i + 1])
                if masked:
                    scores = hide(mask, scores, (group.stop - group.start) // PAIR)
                probs = jnp.exp2(scores)
                dscore = (probs * lean).astype(jnp.bfloat16)
                value_terms += dot(probs.astype(jnp.bfloat16), g_sorted[pair, group, :])
                key_terms += dot(dscore, q_sorted[pair, group, :])
                query_total[pair, :, group] += dot(keys_turned, dscore)
            for i, tile in enumerate(tiles):
                at = slice(i * TILE, (i + 1) * TILE)
                value_total[rows_of(tile), :] += value_terms[at]
                key_total[rows_of(tile), :] += key_terms[at]

        walk(order, counts, pair, step)
        return 0

    lax.fori_loop(0, PAIRS, one_pair, 0)

    def unsort_keys(i, _):
        for s in range(2):
            rank = key_rank[2 * i + s]
            at = pl.ds(pl.multiple_of(rank * SPAN, SPAN), SPAN)
            both = jnp.concatenate([key_total[at, :] * SCALE, value_total[at, :]], axis=1)
            kv[i, s * SPAN:(s + 1) * SPAN, :] = both.astype(jnp.bfloat16)
        return 0

    lax.fori_loop(0, PLANE, unsort_keys, 0)
    for pair in range(PAIRS):
        for h in range(HEADS):
            scaled = query_total[pair, :, h * PAIR:(h + 1) * PAIR] * SCALE
            rows[pair, :, h * DIM:(h + 1) * DIM] = jnp.transpose(scaled.astype(jnp.bfloat16))
    give_back(query_rank, rows, outs, WIDTH)


def shape(dims, dtype):
    return jax.ShapeDtypeStruct(dims, dtype)


def cost(matmuls):
    terms = PAIRS * LANES * KEYS // 2
    return pl.CostEstimate(
        flops=2 * matmuls * terms * DIM, bytes_accessed=8 * KEYS * DIM, transcendentals=terms
    )


SMEM = pl.BlockSpec(memory_space=pltpu.SMEM)
VMEM = pl.BlockSpec(memory_space=pltpu.VMEM)
HBM = pl.BlockSpec(memory_space=pltpu.HBM)


def ring(step):
    return [(i, i - i % SIDE + (i + step) % SIDE) for i in range(SIDE**3)]


def plan(mask_ranges, span_ids, place):
    line, z, core = place // SIDE, place % SIDE, lax.axis_index("grp")
    ids = span_ids.reshape(PLANE, SIDE, 2, 2)
    query_ids = jnp.concatenate(
        [ids[line, (z - step) % SIDE, side] for side in (core, 1 - core) for step in SHIFTS]
    )
    key_ids = ids[:, z, core].reshape(KEY_SPANS)

    def ranked(values):
        rank = jnp.sum((values[None, :] < values[:, None]).astype(jnp.int32), axis=1)
        at = jnp.arange(values.shape[0], dtype=jnp.int32)
        hit = (rank[:, None] == at[None, :]).astype(jnp.int32)
        return rank, jnp.sum(hit * values[:, None], axis=0)

    query_rank, query_sorted = ranked(query_ids)
    key_rank, key_sorted = ranked(key_ids)
    q_from, q_to, k_from, k_to, kind = [mask_ranges[:, column] for column in range(5)]
    q_low = jnp.maximum(query_sorted[:, None] * SPAN, q_from)
    q_high = jnp.minimum(query_sorted[:, None] * SPAN + SPAN, q_to)
    k_low = jnp.maximum(key_sorted[:, None] * SPAN, k_from)
    k_high = jnp.minimum(key_sorted[:, None] * SPAN + SPAN, k_to)
    some = (q_low < q_high)[:, None, :] & (k_low < k_high)[None, :, :]
    some = some & ((kind == 1) | (k_low[None, :, :] < q_high[:, None, :]))
    whole = (
        (q_high - q_low == SPAN)[:, None, :]
        & (k_high - k_low == SPAN)[None, :, :]
        & ((kind == 1) | (k_high[None, :, :] <= q_low[:, None, :] + 1))
    )
    by_tile = (PAIRS, 2, TILES, TILE_SPANS)
    some = jnp.any(some, axis=2).reshape(by_tile).any(axis=(1, 3))
    whole = jnp.any(whole, axis=2).reshape(by_tile).all(axis=(1, 3))
    tile_at = jnp.arange(TILES, dtype=jnp.int32)
    key = jnp.where(whole, 0, jnp.where(some, TILES, 2 * TILES)) + tile_at
    rank = jnp.sum((key[:, None, :] < key[:, :, None]).astype(jnp.int32), axis=2)
    order = jnp.sum(
        jnp.where(rank[:, :, None] == tile_at, tile_at[:, None], 0), axis=1
    ).reshape(PAIRS * TILES)
    counts = jnp.stack(
        [jnp.sum(which.astype(jnp.int32), axis=1) for which in (whole, some)], axis=1
    ).reshape(2 * PAIRS)
    columns = jnp.stack([k_from, k_to, q_from, q_to, kind])
    ranges = jnp.pad(columns, ((0, 3), (0, PAIR - kind.shape[0])))
    return order, counts, key_sorted, key_rank, query_sorted, query_rank, ranges


def kernel(body, name, scalars, operands, outs, scratch=(), matmuls=0, mebibytes=16, place=VMEM):
    return pl.pallas_call(
        body,
        out_shape=tuple(shape(*out) for out in outs),
        in_specs=[SMEM] * len(scalars) + [place] * len(operands),
        out_specs=(VMEM,) * len(outs),
        scratch_shapes=[pltpu.VMEM(*one) if isinstance(one, tuple) else one for one in scratch],
        compiler_params=pltpu.CompilerParams(vmem_limit_bytes=mebibytes * 1024 * 1024),
        cost_estimate=cost(matmuls) if matmuls else None,
        name=name,
    )(*scalars, *operands)


def per_device(queries, attn_keys, attn_values, out_grad, mask_ranges, span_ids):
    bf16, f32 = jnp.bfloat16, jnp.float32
    place = lax.axis_index("cp")
    planes = [[i * SIDE + z for i in range(PLANE)] for z in range(SIDE)]

    def swap(array):
        return lax.ppermute(array, "grp", [(0, 1), (1, 0)])

    def around(array, sign=1):
        return [lax.ppermute(array, "cp", ring(sign * step)) for step in SHIFTS[1:]]

    def plane_exchange(array):
        return lax.all_to_all(array, "cp", 0, 0, axis_index_groups=planes)

    sorted_shape = ((PAIRS, LANES, DIM), bf16)
    keys_shape = ((KEYS, DIM), bf16)
    kv_shape = ((PLANE, PAIR, 2 * DIM), bf16)
    line_shape = ((PAIR, 2 * WIDTH), bf16)
    lines_shape = ((SIDE, PAIR, 2 * WIDTH), bf16)
    tiles_shape = ((TILES, DIM, TILE), bf16)
    stat_shape = ((STAT_ROWS, LANES), f32)
    feature_shapes = [((PAIRS, PAIR, PAIR), bf16), ((PAIRS, 8, PAIR), jnp.int32)]

    qg, kv_copies = kernel(
        pack_kernel, "pack", [], [queries, out_grad, attn_keys, attn_values],
        [line_shape, kv_shape], [((PAIR, 2 * DIM), bf16), pltpu.SemaphoreType.DMA((4,))],
        mebibytes=60, place=HBM,
    )
    qg_parts = [qg] + around(qg)
    kv = plane_exchange(kv_copies)
    qg_parts += [swap(part) for part in qg_parts]
    order, counts, key_ids, key_rank, query_ids, query_rank, ranges = plan(
        mask_ranges, span_ids, place
    )
    lists = [order, counts, key_ids, key_rank, query_ids, query_rank]
    total, top, stat, q_sorted, g_sorted, k_sorted, v_sorted = kernel(
        forward_kernel, "forward", lists, [*qg_parts, kv, ranges],
        [((PAIRS, DIM, LANES), f32), ((PAIRS, LANES), f32), stat_shape, *[sorted_shape] * 2, *[keys_shape] * 2],
        [tiles_shape, ((8, LANES), f32), *feature_shapes],
        matmuls=2,
    )
    (k_turned,) = kernel(turn_kernel, "turn", [], [k_sorted], [tiles_shape])
    (stat_mine,) = kernel(merge_kernel, "merge", [], [stat, *around(stat)], [stat_shape])
    od_mine, od_other, kv_grad = kernel(
        backward_kernel, "backward", lists,
        [
            q_sorted, g_sorted, k_sorted, v_sorted, k_turned, ranges,
            top, stat_mine, swap(stat_mine), total,
        ],
        [lines_shape, lines_shape, kv_shape],
        [
            *[((KEYS, DIM), f32)] * 2, ((PAIRS, DIM, LANES), f32), ((PAIRS, PAIR, WIDTH), bf16),
            ((PAIRS, 8, LANES), f32), *feature_shapes,
        ],
        matmuls=5, mebibytes=28,
    )
    kv_terms = plane_exchange(kv_grad)
    od_other = swap(od_other)
    home = list(kernel(join_kernel, "join", [], [od_mine, od_other], [line_shape] * SIDE))
    home[1:] = [
        lax.ppermute(part, "cp", ring(-step)) for part, step in zip(home[1:], SHIFTS[1:])
    ]
    return kernel(
        finish_kernel, "finish", [], [*home, kv_terms],
        [((PAIR, WIDTH), bf16)] * 2 + [((PAIR, DIM), bf16)] * 2,
    )


def solution(mesh):
    rows = P(("cp", "grp"), None)
    return jax.shard_map(
        per_device,
        mesh=mesh,
        in_specs=(rows, rows, rows, rows, P(), P()),
        out_specs=(rows, rows, rows, rows),
        check_vma=False,
    )
```

profile of v0, /device:TPU:2, one launch (start us, length us, event | category | flops | bytes accessed | tf_op | source)
XLA Modules:
  0.0 106.9 jit_solution(6172571283669907982)
XLA Ops:
  0.7 2.2 %pack.1 = (bf16[128,1280]{1,0:T(8,128)(2,1)}, bf16[16,128,256]{2,1,0:T(8,128)(2,1)}) custom-call(bf16[128,640]{1,0:T(8,128)(2,1)} %queries.1, bf16[128,640]{1,0:T(8,128)(2,1)} %out_grad.1, bf16[128,128]{1,0:T(8,128)(2,1)} %keys.1, bf16[128,128]{1,0:T(8,128)(2,1)} %values.1), custom_call_target="tpu_custom_call" | custom-call | tf_op jit(solution)/shard_map/pack/pallas_call | solution.py:370
  2.9 4.0 %collective-permute-start.2 = (bf16[128,1280]{1,0:T(8,128)(2,1)}, bf16[128,1280]{1,0:T(8,128)(2,1)S(1)}, u32[]{:S(2)}, u32[]{:S(2)}) collective-permute-start(bf16[128,1280]{1,0:T(8,128)(2,1)} %get-tuple-element.20.qg0), channel_id=1, source_target_pairs={{0,4},{2,6},{4,0},{6,2},{8,12},{10,14},{12,8},{14,10},{16,20},{18,... | collective-permute-start | bytes 983048 | tf_op jit(solution)/shard_map/ppermute | solution.py:391
  6.9 0.7 collective-permute-start.1
  7.6 1.3 %collective-permute-start = (bf16[128,1280]{1,0:T(8,128)(2,1)}, bf16[128,1280]{1,0:T(8,128)(2,1)S(1)}, u32[]{:S(2)}, u32[]{:S(2)}) collective-permute-start(bf16[128,1280]{1,0:T(8,128)(2,1)} %get-tuple-element.20.qg0), channel_id=1, source_target_pairs={{0,2},{2,4},{4,6},{6,0},{8,10},{10,12},{12,14},{14,8},{16,18},{18,... | collective-permute-start | bytes 983048 | tf_op jit(solution)/shard_map/ppermute | solution.py:391
  8.9 7.6 %all-to-all-start = ((bf16[16,128,256]{2,1,0:T(8,128)(2,1)}), bf16[16,128,256]{2,1,0:T(8,128)(2,1)S(1)}, u32[]{:S(2)}, u32[]{:S(2)}) async-start(bf16[16,128,256]{2,1,0:T(8,128)(2,1)} %get-tuple-element.21), calls=%async_computation | async-start | bytes 2097152 | tf_op jit(solution)/shard_map/all_to_all | solution.py:394
  19.0 4.2 %collective-permute-done.1.qg2 = bf16[128,1280]{1,0:T(8,128)(2,1)S(1)} collective-permute-done((bf16[128,1280]{1,0:T(8,128)(2,1)}, bf16[128,1280]{1,0:T(8,128)(2,1)S(1)}, u32[]{:S(2)}, u32[]{:S(2)}) %collective-permute-start.1) | collective-permute-done | bytes 327712 | tf_op jit(solution)/shard_map/ppermute | solution.py:391
  24.4 0.8 collective-permute-done.5.qg6
  25.4 6.6 %all-to-all-done.kv = bf16[16,128,256]{2,1,0:T(8,128)(2,1)S(1)} async-done(((bf16[16,128,256]{2,1,0:T(8,128)(2,1)}), bf16[16,128,256]{2,1,0:T(8,128)(2,1)S(1)}, u32[]{:S(2)}, u32[]{:S(2)}) %all-to-all-start) | async-done | bytes 1048608 | tf_op jit(solution)/shard_map/all_to_all | solution.py:394
  32.1 17.2 %forward.1 = (f32[8,128,640]{2,1,0:T(8,128)S(1)}, f32[8,640]{1,0:T(8,128)S(1)}, f32[16,640]{1,0:T(8,128)S(1)}, bf16[8,640,128]{2,1,0:T(8,128)(2,1)S(1)}, bf16[8,...) custom-call(s32[128]{0:T(128)S(1)} %reshape.414.order, ...), custom_call_target="tpu_custom_call" | custom-call | flops 2684354560 | bytes 2097152 | tf_op jit(solution)/shard_map/forward/pallas_call | solution.py:370
  49.3 2.0 %collective-permute-start.9 = (f32[16,640]{1,0:T(8,128)S(1)}, f32[16,640]{1,0:T(8,128)S(1)}, u32[]{:S(2)}, u32[]{:S(2)}) collective-permute-start(f32[16,640]{1,0:T(8,128)S(1)} %get-tuple-element.27.s0), channel_id=1, source_target_pairs={{0,4},{2,6},{4,0},{6,2},{8,12},{10,14},{12,8},{14,10},{16,20},{18,... | collective-permute-start | bytes 122888 | tf_op jit(solution)/shard_map/ppermute | solution.py:391
  51.3 1.4 %collective-permute-start.8 = (f32[16,640]{1,0:T(8,128)S(1)}, f32[16,640]{1,0:T(8,128)S(1)}, u32[]{:S(2)}, u32[]{:S(2)}) collective-permute-start(f32[16,640]{1,0:T(8,128)S(1)} %get-tuple-element.27.s0), channel_id=1, source_target_pairs={{0,6},{2,0},{4,2},{6,4},{8,14},{10,8},{12,10},{14,12},{16,22},{18,... | collective-permute-start | bytes 122888 | tf_op jit(solution)/shard_map/ppermute | solution.py:391
  52.7 0.7 collective-permute-start.7
  53.3 1.6 %collective-permute-done.9.s3 = f32[16,640]{1,0:T(8,128)S(1)} collective-permute-done((f32[16,640]{1,0:T(8,128)S(1)}, f32[16,640]{1,0:T(8,128)S(1)}, u32[]{:S(2)}, u32[]{:S(2)}) %collective-permute-start.9) | collective-permute-done | bytes 40992 | tf_op jit(solution)/shard_map/ppermute | solution.py:391
  55.3 2.6 %collective-permute-done.7.s1 = f32[16,640]{1,0:T(8,128)S(1)} collective-permute-done((f32[16,640]{1,0:T(8,128)S(1)}, f32[16,640]{1,0:T(8,128)S(1)}, u32[]{:S(2)}, u32[]{:S(2)}) %collective-permute-start.7) | collective-permute-done | bytes 40992 | tf_op jit(solution)/shard_map/ppermute | solution.py:391
  58.4 1.0 collective-permute-done.10.stat_other
  59.4 21.8 %backward.1 = (bf16[4,128,1280]{2,1,0:T(8,128)(2,1)S(1)}, bf16[4,128,1280]{2,1,0:T(8,128)(2,1)}, bf16[16,128,256]{2,1,0:T(8,128)(2,1)}) custom-call(s32[128]{0:T(128)S(1)} %reshape.414.order, s32[16]{0:T(128)S(1)} %reshape.415.counts, s32[32]{0:T(128)S(1)} %select_reduce_fusion.1.key_ids, s32[32]{0:T(128)S(1)} %convert_reduce_fusion.1.key_rank, ...), custom_call_target="tpu_custom_call" | custom-call | flops 6710886400 | bytes 2097152 | tf_op jit(solution)/shard_map/backward/pallas_call | solution.py:370
  81.2 4.4 %all-to-all-start.1 = ((bf16[16,128,256]{2,1,0:T(8,128)(2,1)}), bf16[16,128,256]{2,1,0:T(8,128)(2,1)S(1)}, u32[]{:S(2)}, u32[]{:S(2)}) async-start(bf16[16,128,256]{2,1,0:T(8,128)(2,1)} %get-tuple-element.35), calls=%async_computation.1 | async-start | bytes 2097152 | tf_op jit(solution)/shard_map/all_to_all | solution.py:394
  85.6 2.1 %join.1 = (bf16[128,1280]{1,0:T(8,128)(2,1)S(1)}, bf16[128,1280]{1,0:T(8,128)(2,1)}, bf16[128,1280]{1,0:T(8,128)(2,1)S(1)}, bf16[128,1280]{1,0:T(8,128)(2,1)S(1)}) custom-call(bf16[4,128,1280]{2,1,0:T(8,128)(2,1)S(1)} %get-tuple-element.29.a, bf16[4,128,1280]{2,1,0:T(8,128)(2,1)} %collective-permute-done.11.b), custom_call_target="tpu_custom_call" | custom-call | tf_op jit(solution)/shard_map/join/pallas_call | solution.py:370
  87.7 0.8 collective-permute-start.12
  88.5 1.3 %collective-permute-start.13 = (bf16[128,1280]{1,0:T(8,128)(2,1)S(1)}, bf16[128,1280]{1,0:T(8,128)(2,1)S(1)}, u32[]{:S(2)}, u32[]{:S(2)}) collective-permute-start(bf16[128,1280]{1,0:T(8,128)(2,1)S(1)} %get-tuple-element.33), channel_id=1, source_target_pairs={{0,2},{2,4},{4,6},{6,0},{8,10},{10,12},{12,14},{14,8},{16,18},{18,... | collective-permute-start | bytes 983048 | tf_op jit(solution)/shard_map/ppermute | solution.py:442
  89.7 2.1 %collective-permute-start.14 = (bf16[128,1280]{1,0:T(8,128)(2,1)S(1)}, bf16[128,1280]{1,0:T(8,128)(2,1)S(1)}, u32[]{:S(2)}, u32[]{:S(2)}) collective-permute-start(bf16[128,1280]{1,0:T(8,128)(2,1)S(1)} %get-tuple-element.34), channel_id=1, source_target_pairs={{0,4},{2,6},{4,0},{6,2},{8,12},{10,14},{12,8},{14,10},{16,20},{18,... | collective-permute-start | bytes 983048 | tf_op jit(solution)/shard_map/ppermute | solution.py:442
  91.8 10.3 %all-to-all-done.1.terms = bf16[16,128,256]{2,1,0:T(8,128)(2,1)S(1)} async-done(((bf16[16,128,256]{2,1,0:T(8,128)(2,1)}), bf16[16,128,256]{2,1,0:T(8,128)(2,1)S(1)}, u32[]{:S(2)}, u32[]{:S(2)}) %all-to-all-start.1) | async-done | bytes 1048608 | tf_op jit(solution)/shard_map/all_to_all | solution.py:394
  102.1 4.0 %collective-permute-done.13.a2 = bf16[128,1280]{1,0:T(8,128)(2,1)S(1)} collective-permute-done((bf16[128,1280]{1,0:T(8,128)(2,1)S(1)}, bf16[128,1280]{1,0:T(8,128)(2,1)S(1)}, u32[]{:S(2)}, u32[]{:S(2)}) %collective-permute-start.13) | collective-permute-done | bytes 327712 | tf_op jit(solution)/shard_map/ppermute | solution.py:442
  106.0 0.9 finish.1
  (54 shorter events, 4.7 us)
Async XLA Ops:
  0.6 15.9 %copy-start.1 = (s32[13,5]{0,1:T(8,128)S(1)}, s32[13,5]{0,1:T(8,128)}, u32[]{:S(2)}) copy-start(s32[13,5]{0,1:T(8,128)} %param.10) | copy-start | bytes 784
  0.6 15.9 %copy-start.2 = (s32[256]{0:T(256)S(1)}, s32[256]{0:T(256)}, u32[]{:S(2)}) copy-start(s32[256]{0:T(256)} %param.11) | copy-start | bytes 3076
  2.9 21.5 %collective-permute-start.3 = (bf16[128,1280]{1,0:T(8,128)(2,1)}, bf16[128,1280]{1,0:T(8,128)(2,1)S(1)}, u32[]{:S(2)}, u32[]{:S(2)}) collective-permute-start(bf16[128,1280]{1,0:T(8,128)(2,1)} %get-tuple-element.20.qg0), channel_id=1, source_target_pairs={{0,1},{1,0},{2,3},{3,2},{4,5},{5,4},{6,7},{7,6},{8,9},{9,8},{10,11... | collective-permute-start | bytes 983048 | tf_op jit(solution)/shard_map/ppermute | solution.py:388
  2.9 16.0 %collective-permute-start.2 = (bf16[128,1280]{1,0:T(8,128)(2,1)}, bf16[128,1280]{1,0:T(8,128)(2,1)S(1)}, u32[]{:S(2)}, u32[]{:S(2)}) collective-permute-start(bf16[128,1280]{1,0:T(8,128)(2,1)} %get-tuple-element.20.qg0), channel_id=1, source_target_pairs={{0,4},{2,6},{4,0},{6,2},{8,12},{10,14},{12,8},{14,10},{16,20},{18,... | collective-permute-start | bytes 983048 | tf_op jit(solution)/shard_map/ppermute | solution.py:391
  6.9 16.3 %collective-permute-start.1 = (bf16[128,1280]{1,0:T(8,128)(2,1)}, bf16[128,1280]{1,0:T(8,128)(2,1)S(1)}, u32[]{:S(2)}, u32[]{:S(2)}) collective-permute-start(bf16[128,1280]{1,0:T(8,128)(2,1)} %get-tuple-element.20.qg0), channel_id=1, source_target_pairs={{0,6},{2,0},{4,2},{6,4},{8,14},{10,8},{12,10},{14,12},{16,22},{18,... | collective-permute-start | bytes 983048 | tf_op jit(solution)/shard_map/ppermute | solution.py:391
  7.6 15.6 %collective-permute-start = (bf16[128,1280]{1,0:T(8,128)(2,1)}, bf16[128,1280]{1,0:T(8,128)(2,1)S(1)}, u32[]{:S(2)}, u32[]{:S(2)}) collective-permute-start(bf16[128,1280]{1,0:T(8,128)(2,1)} %get-tuple-element.20.qg0), channel_id=1, source_target_pairs={{0,2},{2,4},{4,6},{6,0},{8,10},{10,12},{12,14},{14,8},{16,18},{18,... | collective-permute-start | bytes 983048 | tf_op jit(solution)/shard_map/ppermute | solution.py:391
  8.9 23.2 %copy-start = (bf16[128,1280]{1,0:T(8,128)(2,1)S(1)}, bf16[128,1280]{1,0:T(8,128)(2,1)}, u32[]{:S(2)}) copy-start(bf16[128,1280]{1,0:T(8,128)(2,1)} %get-tuple-element.20.qg0) | copy-start | bytes 983044
  8.9 23.2 %all-to-all-start = ((bf16[16,128,256]{2,1,0:T(8,128)(2,1)}), bf16[16,128,256]{2,1,0:T(8,128)(2,1)S(1)}, u32[]{:S(2)}, u32[]{:S(2)}) async-start(bf16[16,128,256]{2,1,0:T(8,128)(2,1)} %get-tuple-element.21), calls=%async_computation | async-start | bytes 2097152 | tf_op jit(solution)/shard_map/all_to_all | solution.py:394
  18.9 5.4 %collective-permute-start.6 = (bf16[128,1280]{1,0:T(8,128)(2,1)S(1)}, bf16[128,1280]{1,0:T(8,128)(2,1)S(1)}, u32[]{:S(2)}, u32[]{:S(2)}) collective-permute-start(bf16[128,1280]{1,0:T(8,128)(2,1)S(1)} %collective-permute-done.2.qg3), channel_id=1, source_target_pairs={{0,1},{1,0},{2,3},{3,2},{4,5},{5,4},{6,7},{7,6},{8,9},{9,8},{10,11... | collective-permute-start | bytes 983048 | tf_op jit(solution)/shard_map/ppermute | solution.py:388
  23.2 2.0 %collective-permute-start.5 = (bf16[128,1280]{1,0:T(8,128)(2,1)S(1)}, bf16[128,1280]{1,0:T(8,128)(2,1)S(1)}, u32[]{:S(2)}, u32[]{:S(2)}) collective-permute-start(bf16[128,1280]{1,0:T(8,128)(2,1)S(1)} %collective-permute-done.1.qg2), channel_id=1, source_target_pairs={{0,1},{1,0},{2,3},{3,2},{4,5},{5,4},{6,7},{7,6},{8,9},{9,8},{10,11... | collective-permute-start | bytes 983048 | tf_op jit(solution)/shard_map/ppermute | solution.py:388
  23.2 2.2 %collective-permute-start.4 = (bf16[128,1280]{1,0:T(8,128)(2,1)S(1)}, bf16[128,1280]{1,0:T(8,128)(2,1)}, u32[]{:S(2)}, u32[]{:S(2)}) collective-permute-start(bf16[128,1280]{1,0:T(8,128)(2,1)S(1)} %collective-permute-done.qg1), channel_id=1, source_target_pairs={{0,1},{1,0},{2,3},{3,2},{4,5},{5,4},{6,7},{7,6},{8,9},{9,8},{10,11... | collective-permute-start | bytes 983048 | tf_op jit(solution)/shard_map/ppermute | solution.py:388
  49.3 5.6 %collective-permute-start.9 = (f32[16,640]{1,0:T(8,128)S(1)}, f32[16,640]{1,0:T(8,128)S(1)}, u32[]{:S(2)}, u32[]{:S(2)}) collective-permute-start(f32[16,640]{1,0:T(8,128)S(1)} %get-tuple-element.27.s0), channel_id=1, source_target_pairs={{0,4},{2,6},{4,0},{6,2},{8,12},{10,14},{12,8},{14,10},{16,20},{18,... | collective-permute-start | bytes 122888 | tf_op jit(solution)/shard_map/ppermute | solution.py:391
  51.3 4.0 %collective-permute-start.8 = (f32[16,640]{1,0:T(8,128)S(1)}, f32[16,640]{1,0:T(8,128)S(1)}, u32[]{:S(2)}, u32[]{:S(2)}) collective-permute-start(f32[16,640]{1,0:T(8,128)S(1)} %get-tuple-element.27.s0), channel_id=1, source_target_pairs={{0,6},{2,0},{4,2},{6,4},{8,14},{10,8},{12,10},{14,12},{16,22},{18,... | collective-permute-start | bytes 122888 | tf_op jit(solution)/shard_map/ppermute | solution.py:391
  52.7 5.2 %collective-permute-start.7 = (f32[16,640]{1,0:T(8,128)S(1)}, f32[16,640]{1,0:T(8,128)S(1)}, u32[]{:S(2)}, u32[]{:S(2)}) collective-permute-start(f32[16,640]{1,0:T(8,128)S(1)} %get-tuple-element.27.s0), channel_id=1, source_target_pairs={{0,2},{2,4},{4,6},{6,0},{8,10},{10,12},{12,14},{14,8},{16,18},{18,... | collective-permute-start | bytes 122888 | tf_op jit(solution)/shard_map/ppermute | solution.py:391
  57.9 1.5 %collective-permute-start.10 = (f32[16,640]{1,0:T(8,128)S(1)}, f32[16,640]{1,0:T(8,128)S(1)}, u32[]{:S(2)}, u32[]{:S(2)}) collective-permute-start(f32[16,640]{1,0:T(8,128)S(1)} %merge.1.stat_mine), channel_id=1, source_target_pairs={{0,1},{1,0},{2,3},{3,2},{4,5},{5,4},{6,7},{7,6},{8,9},{9,8},{10,11... | collective-permute-start | bytes 122888 | tf_op jit(solution)/shard_map/ppermute | solution.py:388
  81.2 4.4 %collective-permute-start.11 = (bf16[4,128,1280]{2,1,0:T(8,128)(2,1)}, bf16[4,128,1280]{2,1,0:T(8,128)(2,1)}, u32[]{:S(2)}, u32[]{:S(2)}) collective-permute-start(bf16[4,128,1280]{2,1,0:T(8,128)(2,1)} %get-tuple-element.30), channel_id=1, source_target_pairs={{0,1},{1,0},{2,3},{3,2},{4,5},{5,4},{6,7},{7,6},{8,9},{9,8},{10,11... | collective-permute-start | bytes 3932168 | tf_op jit(solution)/shard_map/ppermute | solution.py:388
  81.2 20.9 %all-to-all-start.1 = ((bf16[16,128,256]{2,1,0:T(8,128)(2,1)}), bf16[16,128,256]{2,1,0:T(8,128)(2,1)S(1)}, u32[]{:S(2)}, u32[]{:S(2)}) async-start(bf16[16,128,256]{2,1,0:T(8,128)(2,1)} %get-tuple-element.35), calls=%async_computation.1 | async-start | bytes 2097152 | tf_op jit(solution)/shard_map/all_to_all | solution.py:394
  87.7 14.4 %collective-permute-start.12 = (bf16[128,1280]{1,0:T(8,128)(2,1)}, bf16[128,1280]{1,0:T(8,128)(2,1)S(1)}, u32[]{:S(2)}, u32[]{:S(2)}) collective-permute-start(bf16[128,1280]{1,0:T(8,128)(2,1)} %get-tuple-element.32), channel_id=1, source_target_pairs={{0,6},{2,0},{4,2},{6,4},{8,14},{10,8},{12,10},{14,12},{16,22},{18,... | collective-permute-start | bytes 983048 | tf_op jit(solution)/shard_map/ppermute | solution.py:442
  88.5 17.5 %collective-permute-start.13 = (bf16[128,1280]{1,0:T(8,128)(2,1)S(1)}, bf16[128,1280]{1,0:T(8,128)(2,1)S(1)}, u32[]{:S(2)}, u32[]{:S(2)}) collective-permute-start(bf16[128,1280]{1,0:T(8,128)(2,1)S(1)} %get-tuple-element.33), channel_id=1, source_target_pairs={{0,2},{2,4},{4,6},{6,0},{8,10},{10,12},{12,14},{14,8},{16,18},{18,... | collective-permute-start | bytes 983048 | tf_op jit(solution)/shard_map/ppermute | solution.py:442
  89.7 16.3 %collective-permute-start.14 = (bf16[128,1280]{1,0:T(8,128)(2,1)S(1)}, bf16[128,1280]{1,0:T(8,128)(2,1)S(1)}, u32[]{:S(2)}, u32[]{:S(2)}) collective-permute-start(bf16[128,1280]{1,0:T(8,128)(2,1)S(1)} %get-tuple-element.34), channel_id=1, source_target_pairs={{0,4},{2,6},{4,0},{6,2},{8,12},{10,14},{12,8},{14,10},{16,20},{18,... | collective-permute-start | bytes 983048 | tf_op jit(solution)/shard_map/ppermute | solution.py:442
where the time goes:
time: 105 us; the launch traced here: 107 us
  Pallas kernels  44.4 us (42%)
  waiting for transfers between devices  31.7 us (30%)
  starting transfers between devices  27.1 us (26%)
  other arithmetic  2.05 us (2%)
    pallas_call x7, Pallas kernels, kernel(): pl.pallas_call(body, out_shape=tuple((shape(*out) for out in outs)), in_s...  44.4 us
    all_to_all x2, waiting for transfers between devices, plane_exchange(): return lax.all_to_all(array, 'cp', 0, 0, axis_index_groups=planes)  16.9 us
    all_to_all x2, starting transfers between devices, plane_exchange(): return lax.all_to_all(array, 'cp', 0, 0, axis_index_groups=planes)  12 us
    ppermute x6, starting transfers between devices, around(): return [lax.ppermute(array, 'cp', ring(sign * step)) for step in SHIFTS[1:]]  10 us
    ppermute x6, waiting for transfers between devices, around(): return [lax.ppermute(array, 'cp', ring(sign * step)) for step in SHIFTS[1:]]  8.72 us
    ppermute x3, starting transfers between devices, per_device(): lax.ppermute(part, 'cp', ring(-step))  4.09 us
    ppermute x3, waiting for transfers between devices, per_device(): lax.ppermute(part, 'cp', ring(-step))  3.97 us
  transfers between devices with their start and end apart: 17, of which 10 were waited for; matrix products, arithmetic and copies ran while one was open for 3% of the time, Pallas kernels for 2%

commit v1 on v0

--- a/solution.py
+++ b/solution.py
@@ -25,6 +25,7 @@
 WIDTH = HEADS * DIM
 GROUPS = (slice(0, 256), slice(256, 512), slice(512, 640))
 FAR = -1e30
+SAFE_LOG = 60.0
 SCALE = 1.0 / math.sqrt(DIM)
 LOG2_SCALE = SCALE * math.log2(math.e)
 SHIFTS = (0, 1, -1, 2)
@@ -64,6 +65,11 @@
         weight = jnp.where(ranges[4:5, :] == 1, 64.0, 1.0)
         query_feature[pair] = flip(jnp.where(holds, weight, 0.0)).astype(jnp.bfloat16)
         query_at[pair] = jnp.transpose(at)[0:8, :]
+
+
+def largest_norm(rows):
+    sums = dot(rows * rows, jnp.ones((DIM, DIM), jnp.bfloat16))
+    return jnp.max(sums.reshape(rows.shape[0] // 8, 8, DIM), axis=0)
 
 
 def walk(order, counts, pair, step):
@@ -157,9 +163,13 @@
     for t in range(TILES):
         v_turned[t] = jnp.transpose(v_sorted[t * TILE:(t + 1) * TILE, :])
 
-    def one_pair(pair, _):
+    query_norm = functools.reduce(jnp.maximum, [largest_norm(q_sorted[p]) for p in range(PAIRS)])
+    norms = [jnp.max(norm, axis=0, keepdims=True) for norm in (query_norm, largest_norm(k_sorted[...]))]
+    small = jnp.max(norms[0] * norms[1]) * (1.02 * LOG2_SCALE**2) <= SAFE_LOG**2
+
+    def one_pair(bounded, pair, _):
         total_out[pair] = jnp.zeros((DIM, LANES), jnp.float32)
-        stat[0:1, :] = jnp.full((1, LANES), FAR, jnp.float32)
+        stat[0:1, :] = jnp.full((1, LANES), 0.0 if bounded else FAR, jnp.float32)
         stat[1:2, :] = jnp.zeros((1, LANES), jnp.float32)
 
         def step(masked, tiles):
@@ -174,15 +184,17 @@
                     raw = dot(keys, q_sorted[pair, GROUPS[i + 1], :], NT)
                 if masked:
                     scores = hide(mask, scores, (group.stop - group.start) // PAIR)
-                old = stat[0:1, group]
-                new = jnp.maximum(old, jnp.max(scores, axis=0, keepdims=True))
-                terms = jnp.exp2(scores - new)
-                fade = jnp.exp2(old - new)
-                stat[0:1, group] = new
-                stat[1:2, group] = stat[1:2, group] * fade + jnp.sum(terms, axis=0, keepdims=True)
-                total_out[pair, :, group] = total_out[pair, :, group] * fade + dot(
-                    values, terms.astype(jnp.bfloat16)
-                )
+                mass, total = stat[1:2, group], total_out[pair, :, group]
+                if not bounded:
+                    old = stat[0:1, group]
+                    new = jnp.maximum(old, jnp.max(scores, axis=0, keepdims=True))
+                    scores = scores - new
+                    fade = jnp.exp2(old - new)
+                    stat[0:1, group] = new
+                    mass, total = mass * fade, total * fade
+                terms = jnp.exp2(scores)
+                stat[1:2, group] = mass + jnp.sum(terms, axis=0, keepdims=True)
+                total_out[pair, :, group] = total + dot(values, terms.astype(jnp.bfloat16))
 
         walk(order, counts, pair, step)
         for h in range(HEADS):
@@ -195,7 +207,13 @@
         stat_out[pl.ds(PAIRS + pair, 1), :] = stat[2:3, :] / mass
         return 0
 
-    lax.fori_loop(0, PAIRS, one_pair, 0)
+    @pl.when(small)
+    def _():
+        lax.fori_loop(0, PAIRS, functools.partial(one_pair, True), 0)
+
+    @pl.when(jnp.logical_not(small))
+    def _():
+        lax.fori_loop(0, PAIRS, functools.partial(one_pair, False), 0)
 
 
 def merge(parts):

time: 105 us -> 101 us (0.962); the launches traced: 107 us -> 100 us
  Pallas kernels: 44.4 us -> 35.9 us
  starting transfers between devices: 27.1 us -> 28.2 us
    pallas_call x7, Pallas kernels: 44.4 us -> 35.9 us  [kernel(): pl.pallas_call(body, out_shape=tuple((shape(*out) for out in outs)), in_s...]
    all_to_all x2, starting transfers between devices: 12 us -> 15.3 us  [plane_exchange(): return lax.all_to_all(array, 'cp', 0, 0, axis_index_groups=planes)]
    all_to_all x2, waiting for transfers between devices: 16.9 us -> 18.3 us  [plane_exchange(): return lax.all_to_all(array, 'cp', 0, 0, axis_index_groups=planes)]
    ppermute x6, starting transfers between devices: 10 us -> 8.86 us  [around(): return [lax.ppermute(array, 'cp', ring(sign * step)) for step in SHIFTS[1:]]]
  transfers between devices with their start and end apart: 17 -> 17, of which waited for: 10 -> 9; matrix products, arithmetic and copies ran while one was open for 3% -> 3% of each run, Pallas kernels for 2% -> 2%
where the time goes in v1:
time: 101 us; the launch traced here: 100 us
  Pallas kernels  35.9 us (36%)
  waiting for transfers between devices  32.3 us (32%)
  starting transfers between devices  28.2 us (28%)
  other arithmetic  2.05 us (2%)
    pallas_call x7, Pallas kernels, kernel(): pl.pallas_call(body, out_shape=tuple((shape(*out) for out in outs)), in_s...  35.9 us
    all_to_all x2, waiting for transfers between devices, plane_exchange(): return lax.all_to_all(array, 'cp', 0, 0, axis_index_groups=planes)  18.3 us
    all_to_all x2, starting transfers between devices, plane_exchange(): return lax.all_to_all(array, 'cp', 0, 0, axis_index_groups=planes)  15.3 us
    ppermute x6, starting transfers between devices, around(): return [lax.ppermute(array, 'cp', ring(sign * step)) for step in SHIFTS[1:]]  8.86 us
    ppermute x6, waiting for transfers between devices, around(): return [lax.ppermute(array, 'cp', ring(sign * step)) for step in SHIFTS[1:]]  8.61 us
    ppermute x3, waiting for transfers between devices, per_device(): lax.ppermute(part, 'cp', ring(-step))  3.28 us
    ppermute x3, starting transfers between devices, per_device(): lax.ppermute(part, 'cp', ring(-step))  3.09 us
    ppermute x6, waiting for transfers between devices, swap(): return lax.ppermute(array, 'grp', [(0, 1), (1, 0)])  2.07 us
  transfers between devices with their start and end apart: 17, of which 9 were waited for; matrix products, arithmetic and copies ran while one was open for 3% of the time, Pallas kernels for 2%

profile of v1, /device:TPU:2, one launch (start us, length us, event | category | flops | bytes accessed | tf_op | source)
XLA Modules:
  0.0 100.2 jit_solution(17135060476727079306)
XLA Ops:
  0.7 2.2 %pack.1 = (bf16[128,1280]{1,0:T(8,128)(2,1)}, bf16[16,128,256]{2,1,0:T(8,128)(2,1)}) custom-call(bf16[128,640]{1,0:T(8,128)(2,1)} %queries.1, bf16[128,640]{1,0:T(8,128)(2,1)} %out_grad.1, bf16[128,128]{1,0:T(8,128)(2,1)} %keys.1, bf16[128,128]{1,0:T(8,128)(2,1)} %values.1), custom_call_target="tpu_custom_call" | custom-call | tf_op jit(solution)/shard_map/pack/pallas_call | solution.py:388
  2.9 4.0 %collective-permute-start.2 = (bf16[128,1280]{1,0:T(8,128)(2,1)}, bf16[128,1280]{1,0:T(8,128)(2,1)S(1)}, u32[]{:S(2)}, u32[]{:S(2)}) collective-permute-start(bf16[128,1280]{1,0:T(8,128)(2,1)} %get-tuple-element.20.qg0), channel_id=1, source_target_pairs={{0,4},{2,6},{4,0},{6,2},{8,12},{10,14},{12,8},{14,10},{16,20},{18,... | collective-permute-start | bytes 983048 | tf_op jit(solution)/shard_map/ppermute | solution.py:409
  6.9 0.7 collective-permute-start.1
  7.6 1.3 %collective-permute-start = (bf16[128,1280]{1,0:T(8,128)(2,1)}, bf16[128,1280]{1,0:T(8,128)(2,1)S(1)}, u32[]{:S(2)}, u32[]{:S(2)}) collective-permute-start(bf16[128,1280]{1,0:T(8,128)(2,1)} %get-tuple-element.20.qg0), channel_id=1, source_target_pairs={{0,2},{2,4},{4,6},{6,0},{8,10},{10,12},{12,14},{14,8},{16,18},{18,... | collective-permute-start | bytes 983048 | tf_op jit(solution)/shard_map/ppermute | solution.py:409
  8.9 7.6 %all-to-all-start = ((bf16[16,128,256]{2,1,0:T(8,128)(2,1)}), bf16[16,128,256]{2,1,0:T(8,128)(2,1)S(1)}, u32[]{:S(2)}, u32[]{:S(2)}) async-start(bf16[16,128,256]{2,1,0:T(8,128)(2,1)} %get-tuple-element.21), calls=%async_computation | async-start | bytes 2097152 | tf_op jit(solution)/shard_map/all_to_all | solution.py:412
  19.0 4.2 %collective-permute-done.1.qg2 = bf16[128,1280]{1,0:T(8,128)(2,1)S(1)} collective-permute-done((bf16[128,1280]{1,0:T(8,128)(2,1)}, bf16[128,1280]{1,0:T(8,128)(2,1)S(1)}, u32[]{:S(2)}, u32[]{:S(2)}) %collective-permute-start.1) | collective-permute-done | bytes 327712 | tf_op jit(solution)/shard_map/ppermute | solution.py:409
  23.2 0.5 collective-permute-start.4
  24.4 0.8 collective-permute-done.5.qg6
  25.4 6.6 %all-to-all-done.kv = bf16[16,128,256]{2,1,0:T(8,128)(2,1)S(1)} async-done(((bf16[16,128,256]{2,1,0:T(8,128)(2,1)}), bf16[16,128,256]{2,1,0:T(8,128)(2,1)S(1)}, u32[]{:S(2)}, u32[]{:S(2)}) %all-to-all-start) | async-done | bytes 1048608 | tf_op jit(solution)/shard_map/all_to_all | solution.py:412
  32.1 13.8 %forward.1 = (f32[8,128,640]{2,1,0:T(8,128)S(1)}, f32[8,640]{1,0:T(8,128)S(1)}, f32[16,640]{1,0:T(8,128)S(1)}, bf16[8,640,128]{2,1,0:T(8,128)(2,1)S(1)}, bf16[8,...) custom-call(s32[128]{0:T(128)S(1)} %reshape.414.order, ...), custom_call_target="tpu_custom_call" | custom-call | flops 2684354560 | bytes 2097152 | tf_op jit(solution)/shard_map/forward/pallas_call | solution.py:388
  45.9 0.5 collective-permute-start.9
  46.3 1.6 %collective-permute-start.8 = (f32[16,640]{1,0:T(8,128)S(1)}, f32[16,640]{1,0:T(8,128)S(1)}, u32[]{:S(2)}, u32[]{:S(2)}) collective-permute-start(f32[16,640]{1,0:T(8,128)S(1)} %get-tuple-element.27.s0), channel_id=1, source_target_pairs={{0,6},{2,0},{4,2},{6,4},{8,14},{10,8},{12,10},{14,12},{16,22},{18,... | collective-permute-start | bytes 122888 | tf_op jit(solution)/shard_map/ppermute | solution.py:409
  48.0 0.8 collective-permute-start.7
  48.7 2.7 %collective-permute-done.9.s3 = f32[16,640]{1,0:T(8,128)S(1)} collective-permute-done((f32[16,640]{1,0:T(8,128)S(1)}, f32[16,640]{1,0:T(8,128)S(1)}, u32[]{:S(2)}, u32[]{:S(2)}) %collective-permute-start.9) | collective-permute-done | bytes 40992 | tf_op jit(solution)/shard_map/ppermute | solution.py:409
  51.5 1.7 %collective-permute-done.7.s1 = f32[16,640]{1,0:T(8,128)S(1)} collective-permute-done((f32[16,640]{1,0:T(8,128)S(1)}, f32[16,640]{1,0:T(8,128)S(1)}, u32[]{:S(2)}, u32[]{:S(2)}) %collective-permute-start.7) | collective-permute-done | bytes 40992 | tf_op jit(solution)/shard_map/ppermute | solution.py:409
  53.7 1.0 %collective-permute-done.10.stat_other = f32[16,640]{1,0:T(8,128)S(1)} collective-permute-done((f32[16,640]{1,0:T(8,128)S(1)}, f32[16,640]{1,0:T(8,128)S(1)}, u32[]{:S(2)}, u32[]{:S(2)}) %collective-permute-start.10) | collective-permute-done | bytes 40992 | tf_op jit(solution)/shard_map/ppermute | solution.py:406
  54.7 16.7 %backward.1 = (bf16[4,128,1280]{2,1,0:T(8,128)(2,1)S(1)}, bf16[4,128,1280]{2,1,0:T(8,128)(2,1)}, bf16[16,128,256]{2,1,0:T(8,128)(2,1)}) custom-call(s32[128]{0:T(128)S(1)} %reshape.414.order, s32[16]{0:T(128)S(1)} %reshape.415.counts, s32[32]{0:T(128)S(1)} %select_reduce_fusion.1.key_ids, s32[32]{0:T(128)S(1)} %convert_reduce_fusion.1.key_rank, ...), custom_call_target="tpu_custom_call" | custom-call | flops 6710886400 | bytes 2097152 | tf_op jit(solution)/shard_map/backward/pallas_call | solution.py:388
  71.4 7.7 %all-to-all-start.1 = ((bf16[16,128,256]{2,1,0:T(8,128)(2,1)}), bf16[16,128,256]{2,1,0:T(8,128)(2,1)S(1)}, u32[]{:S(2)}, u32[]{:S(2)}) async-start(bf16[16,128,256]{2,1,0:T(8,128)(2,1)} %get-tuple-element.35), calls=%async_computation.1 | async-start | bytes 2097152 | tf_op jit(solution)/shard_map/all_to_all | solution.py:412
  79.1 2.1 %join.1 = (bf16[128,1280]{1,0:T(8,128)(2,1)S(1)}, bf16[128,1280]{1,0:T(8,128)(2,1)}, bf16[128,1280]{1,0:T(8,128)(2,1)S(1)}, bf16[128,1280]{1,0:T(8,128)(2,1)S(1)}) custom-call(bf16[4,128,1280]{2,1,0:T(8,128)(2,1)S(1)} %get-tuple-element.29.a, bf16[4,128,1280]{2,1,0:T(8,128)(2,1)} %collective-permute-done.11.b), custom_call_target="tpu_custom_call" | custom-call | tf_op jit(solution)/shard_map/join/pallas_call | solution.py:388
  81.4 1.8 %collective-permute-start.13 = (bf16[128,1280]{1,0:T(8,128)(2,1)S(1)}, bf16[128,1280]{1,0:T(8,128)(2,1)S(1)}, u32[]{:S(2)}, u32[]{:S(2)}) collective-permute-start(bf16[128,1280]{1,0:T(8,128)(2,1)S(1)} %get-tuple-element.33), channel_id=1, source_target_pairs={{0,2},{2,4},{4,6},{6,0},{8,10},{10,12},{12,14},{14,8},{16,18},{18,... | collective-permute-start | bytes 983048 | tf_op jit(solution)/shard_map/ppermute | solution.py:460
  83.2 1.1 %collective-permute-start.14 = (bf16[128,1280]{1,0:T(8,128)(2,1)S(1)}, bf16[128,1280]{1,0:T(8,128)(2,1)S(1)}, u32[]{:S(2)}, u32[]{:S(2)}) collective-permute-start(bf16[128,1280]{1,0:T(8,128)(2,1)S(1)} %get-tuple-element.34), channel_id=1, source_target_pairs={{0,4},{2,6},{4,0},{6,2},{8,12},{10,14},{12,8},{14,10},{16,20},{18,... | collective-permute-start | bytes 983048 | tf_op jit(solution)/shard_map/ppermute | solution.py:460
  84.3 11.7 %all-to-all-done.1.terms = bf16[16,128,256]{2,1,0:T(8,128)(2,1)S(1)} async-done(((bf16[16,128,256]{2,1,0:T(8,128)(2,1)}), bf16[16,128,256]{2,1,0:T(8,128)(2,1)S(1)}, u32[]{:S(2)}, u32[]{:S(2)}) %all-to-all-start.1) | async-done | bytes 1048608 | tf_op jit(solution)/shard_map/all_to_all | solution.py:412
  96.0 3.3 %collective-permute-done.13.a2 = bf16[128,1280]{1,0:T(8,128)(2,1)S(1)} collective-permute-done((bf16[128,1280]{1,0:T(8,128)(2,1)S(1)}, bf16[128,1280]{1,0:T(8,128)(2,1)S(1)}, u32[]{:S(2)}, u32[]{:S(2)}) %collective-permute-start.13) | collective-permute-done | bytes 327712 | tf_op jit(solution)/shard_map/ppermute | solution.py:460
  99.2 0.9 finish.1
  (54 shorter events, 4.1 us)
Async XLA Ops:
  0.6 15.9 %copy-start.1 = (s32[13,5]{0,1:T(8,128)S(1)}, s32[13,5]{0,1:T(8,128)}, u32[]{:S(2)}) copy-start(s32[13,5]{0,1:T(8,128)} %param.10) | copy-start | bytes 784
  0.6 15.9 %copy-start.2 = (s32[256]{0:T(256)S(1)}, s32[256]{0:T(256)}, u32[]{:S(2)}) copy-start(s32[256]{0:T(256)} %param.11) | copy-start | bytes 3076
  2.9 21.5 %collective-permute-start.3 = (bf16[128,1280]{1,0:T(8,128)(2,1)}, bf16[128,1280]{1,0:T(8,128)(2,1)S(1)}, u32[]{:S(2)}, u32[]{:S(2)}) collective-permute-start(bf16[128,1280]{1,0:T(8,128)(2,1)} %get-tuple-element.20.qg0), channel_id=1, source_target_pairs={{0,1},{1,0},{2,3},{3,2},{4,5},{5,4},{6,7},{7,6},{8,9},{9,8},{10,11... | collective-permute-start | bytes 983048 | tf_op jit(solution)/shard_map/ppermute | solution.py:406
  2.9 16.0 %collective-permute-start.2 = (bf16[128,1280]{1,0:T(8,128)(2,1)}, bf16[128,1280]{1,0:T(8,128)(2,1)S(1)}, u32[]{:S(2)}, u32[]{:S(2)}) collective-permute-start(bf16[128,1280]{1,0:T(8,128)(2,1)} %get-tuple-element.20.qg0), channel_id=1, source_target_pairs={{0,4},{2,6},{4,0},{6,2},{8,12},{10,14},{12,8},{14,10},{16,20},{18,... | collective-permute-start | bytes 983048 | tf_op jit(solution)/shard_map/ppermute | solution.py:409
  6.9 16.3 %collective-permute-start.1 = (bf16[128,1280]{1,0:T(8,128)(2,1)}, bf16[128,1280]{1,0:T(8,128)(2,1)S(1)}, u32[]{:S(2)}, u32[]{:S(2)}) collective-permute-start(bf16[128,1280]{1,0:T(8,128)(2,1)} %get-tuple-element.20.qg0), channel_id=1, source_target_pairs={{0,6},{2,0},{4,2},{6,4},{8,14},{10,8},{12,10},{14,12},{16,22},{18,... | collective-permute-start | bytes 983048 | tf_op jit(solution)/shard_map/ppermute | solution.py:409
  7.6 15.6 %collective-permute-start = (bf16[128,1280]{1,0:T(8,128)(2,1)}, bf16[128,1280]{1,0:T(8,128)(2,1)S(1)}, u32[]{:S(2)}, u32[]{:S(2)}) collective-permute-start(bf16[128,1280]{1,0:T(8,128)(2,1)} %get-tuple-element.20.qg0), channel_id=1, source_target_pairs={{0,2},{2,4},{4,6},{6,0},{8,10},{10,12},{12,14},{14,8},{16,18},{18,... | collective-permute-start | bytes 983048 | tf_op jit(solution)/shard_map/ppermute | solution.py:409
  8.9 23.2 %copy-start = (bf16[128,1280]{1,0:T(8,128)(2,1)S(1)}, bf16[128,1280]{1,0:T(8,128)(2,1)}, u32[]{:S(2)}) copy-start(bf16[128,1280]{1,0:T(8,128)(2,1)} %get-tuple-element.20.qg0) | copy-start | bytes 983044
  8.9 23.2 %all-to-all-start = ((bf16[16,128,256]{2,1,0:T(8,128)(2,1)}), bf16[16,128,256]{2,1,0:T(8,128)(2,1)S(1)}, u32[]{:S(2)}, u32[]{:S(2)}) async-start(bf16[16,128,256]{2,1,0:T(8,128)(2,1)} %get-tuple-element.21), calls=%async_computation | async-start | bytes 2097152 | tf_op jit(solution)/shard_map/all_to_all | solution.py:412
  18.9 5.4 %collective-permute-start.6 = (bf16[128,1280]{1,0:T(8,128)(2,1)S(1)}, bf16[128,1280]{1,0:T(8,128)(2,1)S(1)}, u32[]{:S(2)}, u32[]{:S(2)}) collective-permute-start(bf16[128,1280]{1,0:T(8,128)(2,1)S(1)} %collective-permute-done.2.qg3), channel_id=1, source_target_pairs={{0,1},{1,0},{2,3},{3,2},{4,5},{5,4},{6,7},{7,6},{8,9},{9,8},{10,11... | collective-permute-start | bytes 983048 | tf_op jit(solution)/shard_map/ppermute | solution.py:406
  23.2 2.0 %collective-permute-start.5 = (bf16[128,1280]{1,0:T(8,128)(2,1)S(1)}, bf16[128,1280]{1,0:T(8,128)(2,1)S(1)}, u32[]{:S(2)}, u32[]{:S(2)}) collective-permute-start(bf16[128,1280]{1,0:T(8,128)(2,1)S(1)} %collective-permute-done.1.qg2), channel_id=1, source_target_pairs={{0,1},{1,0},{2,3},{3,2},{4,5},{5,4},{6,7},{7,6},{8,9},{9,8},{10,11... | collective-permute-start | bytes 983048 | tf_op jit(solution)/shard_map/ppermute | solution.py:406
  23.2 2.2 %collective-permute-start.4 = (bf16[128,1280]{1,0:T(8,128)(2,1)S(1)}, bf16[128,1280]{1,0:T(8,128)(2,1)}, u32[]{:S(2)}, u32[]{:S(2)}) collective-permute-start(bf16[128,1280]{1,0:T(8,128)(2,1)S(1)} %collective-permute-done.qg1), channel_id=1, source_target_pairs={{0,1},{1,0},{2,3},{3,2},{4,5},{5,4},{6,7},{7,6},{8,9},{9,8},{10,11... | collective-permute-start | bytes 983048 | tf_op jit(solution)/shard_map/ppermute | solution.py:406
  45.9 5.6 %collective-permute-start.9 = (f32[16,640]{1,0:T(8,128)S(1)}, f32[16,640]{1,0:T(8,128)S(1)}, u32[]{:S(2)}, u32[]{:S(2)}) collective-permute-start(f32[16,640]{1,0:T(8,128)S(1)} %get-tuple-element.27.s0), channel_id=1, source_target_pairs={{0,4},{2,6},{4,0},{6,2},{8,12},{10,14},{12,8},{14,10},{16,20},{18,... | collective-permute-start | bytes 122888 | tf_op jit(solution)/shard_map/ppermute | solution.py:409
  46.3 5.1 %collective-permute-start.8 = (f32[16,640]{1,0:T(8,128)S(1)}, f32[16,640]{1,0:T(8,128)S(1)}, u32[]{:S(2)}, u32[]{:S(2)}) collective-permute-start(f32[16,640]{1,0:T(8,128)S(1)} %get-tuple-element.27.s0), channel_id=1, source_target_pairs={{0,6},{2,0},{4,2},{6,4},{8,14},{10,8},{12,10},{14,12},{16,22},{18,... | collective-permute-start | bytes 122888 | tf_op jit(solution)/shard_map/ppermute | solution.py:409
  48.0 5.2 %collective-permute-start.7 = (f32[16,640]{1,0:T(8,128)S(1)}, f32[16,640]{1,0:T(8,128)S(1)}, u32[]{:S(2)}, u32[]{:S(2)}) collective-permute-start(f32[16,640]{1,0:T(8,128)S(1)} %get-tuple-element.27.s0), channel_id=1, source_target_pairs={{0,2},{2,4},{4,6},{6,0},{8,10},{10,12},{12,14},{14,8},{16,18},{18,... | collective-permute-start | bytes 122888 | tf_op jit(solution)/shard_map/ppermute | solution.py:409
  53.2 1.5 %collective-permute-start.10 = (f32[16,640]{1,0:T(8,128)S(1)}, f32[16,640]{1,0:T(8,128)S(1)}, u32[]{:S(2)}, u32[]{:S(2)}) collective-permute-start(f32[16,640]{1,0:T(8,128)S(1)} %merge.1.stat_mine), channel_id=1, source_target_pairs={{0,1},{1,0},{2,3},{3,2},{4,5},{5,4},{6,7},{7,6},{8,9},{9,8},{10,11... | collective-permute-start | bytes 122888 | tf_op jit(solution)/shard_map/ppermute | solution.py:406
  71.4 7.7 %collective-permute-start.11 = (bf16[4,128,1280]{2,1,0:T(8,128)(2,1)}, bf16[4,128,1280]{2,1,0:T(8,128)(2,1)}, u32[]{:S(2)}, u32[]{:S(2)}) collective-permute-start(bf16[4,128,1280]{2,1,0:T(8,128)(2,1)} %get-tuple-element.30), channel_id=1, source_target_pairs={{0,1},{1,0},{2,3},{3,2},{4,5},{5,4},{6,7},{7,6},{8,9},{9,8},{10,11... | collective-permute-start | bytes 3932168 | tf_op jit(solution)/shard_map/ppermute | solution.py:406
  71.4 24.5 %all-to-all-start.1 = ((bf16[16,128,256]{2,1,0:T(8,128)(2,1)}), bf16[16,128,256]{2,1,0:T(8,128)(2,1)S(1)}, u32[]{:S(2)}, u32[]{:S(2)}) async-start(bf16[16,128,256]{2,1,0:T(8,128)(2,1)} %get-tuple-element.35), calls=%async_computation.1 | async-start | bytes 2097152 | tf_op jit(solution)/shard_map/all_to_all | solution.py:412
  81.2 14.7 %collective-permute-start.12 = (bf16[128,1280]{1,0:T(8,128)(2,1)}, bf16[128,1280]{1,0:T(8,128)(2,1)S(1)}, u32[]{:S(2)}, u32[]{:S(2)}) collective-permute-start(bf16[128,1280]{1,0:T(8,128)(2,1)} %get-tuple-element.32), channel_id=1, source_target_pairs={{0,6},{2,0},{4,2},{6,4},{8,14},{10,8},{12,10},{14,12},{16,22},{18,... | collective-permute-start | bytes 983048 | tf_op jit(solution)/shard_map/ppermute | solution.py:460
  81.4 17.8 %collective-permute-start.13 = (bf16[128,1280]{1,0:T(8,128)(2,1)S(1)}, bf16[128,1280]{1,0:T(8,128)(2,1)S(1)}, u32[]{:S(2)}, u32[]{:S(2)}) collective-permute-start(bf16[128,1280]{1,0:T(8,128)(2,1)S(1)} %get-tuple-element.33), channel_id=1, source_target_pairs={{0,2},{2,4},{4,6},{6,0},{8,10},{10,12},{12,14},{14,8},{16,18},{18,... | collective-permute-start | bytes 983048 | tf_op jit(solution)/shard_map/ppermute | solution.py:460
  83.2 16.0 %collective-permute-start.14 = (bf16[128,1280]{1,0:T(8,128)(2,1)S(1)}, bf16[128,1280]{1,0:T(8,128)(2,1)S(1)}, u32[]{:S(2)}, u32[]{:S(2)}) collective-permute-start(bf16[128,1280]{1,0:T(8,128)(2,1)S(1)} %get-tuple-element.34), channel_id=1, source_target_pairs={{0,4},{2,6},{4,0},{6,2},{8,12},{10,14},{12,8},{14,10},{16,20},{18,... | collective-permute-start | bytes 983048 | tf_op jit(solution)/shard_map/ppermute | solution.py:460
